TPU v7x, 256 devices: a whole 4x4x8 slice. The times are simulated.
256 devices in a mesh: dp: 64 (over y, z, core), mp: 4 (over x).
Axes of the slice: x: 4, y: 4, z: 8, core: 2. Of those that a mesh axis runs over, the one named last changes fastest.
Arguments:
- features: bfloat16 [32768, 8192], P('dp', 'mp'), may hold values from -6 to 6
- up_cotangent: bfloat16 [32768, 14336], P('dp', 'mp'), may hold values from -0.032958984 to 0.032958984
- proj_basis: bfloat16 [8192, 512], P('mp'), may hold values from -0.0625 to 0.0625
- first_moment: float32 [512, 14336], P('dp', 'mp'), may hold values from -3 to 3
- second_moment: float32 [512, 14336], P('dp', 'mp'), may hold values from 0.0001 to 0.01
Outputs:
- weight_update: float32 [8192, 14336], P('dp', 'mp')
- new_first: float32 [512, 14336], P('dp', 'mp')
- new_second: float32 [512, 14336], P('dp', 'mp')
All inputs are finite; a program needn't handle non-finite values.
Results may differ from a plain program's by a relative error of at most 0.0041.
Values may be sent and summed in bfloat16 or wider, within the bound.
A program may use at most 64 MiB of HBM per device.

v0:
```python
import jax
import jax.numpy as jnp
from jax import lax
from jax.sharding import PartitionSpec as P

STEP = 10


def adam_rows(first_moment, second_moment, low_grad):
    new_first = 0.9 * first_moment + 0.1 * low_grad
    new_second = 0.999 * second_moment + 0.001 * low_grad * low_grad
    first_hat = new_first / (1.0 - 0.9**STEP)
    second_hat = new_second / (1.0 - 0.999**STEP)
    direction = (first_hat / (jnp.sqrt(second_hat) + 1e-08)).astype(jnp.bfloat16)
    return (new_first, new_second, direction)


def body(features, up_cotangent, proj_basis, first_moment, second_moment):
    partial_coeffs = jnp.dot(features, proj_basis, preferred_element_type=jnp.float32)
    coeffs = lax.psum(partial_coeffs, "mp").astype(jnp.bfloat16)
    low_grad = lax.psum_scatter(
        lax.dot_general(
            coeffs, up_cotangent, (((0,), (0,)), ((), ())), preferred_element_type=jnp.float32
        ),
        "dp",
        scatter_dimension=0,
        tiled=True,
    )
    new_first, new_second, direction = adam_rows(first_moment, second_moment, low_grad)
    block_rows = proj_basis.shape[0]
    update_rows = block_rows * lax.axis_size("mp") // lax.axis_size("dp")
    first_row = lax.axis_index("dp") * update_rows
    gathered = lax.all_gather(proj_basis, "mp", axis=0, tiled=True)
    local_basis = lax.dynamic_slice_in_dim(gathered, first_row, update_rows, 0)
    backed = jnp.dot(
        local_basis,
        lax.all_gather(direction, "dp", axis=0, tiled=True),
        preferred_element_type=jnp.float32,
    )
    return (0.25 * backed, new_first, new_second)


def solution(mesh):
    return jax.shard_map(
        body,
        mesh=mesh,
        in_specs=(P("dp", "mp"), P("dp", "mp"), P("mp", None), P("dp", "mp"), P("dp", "mp")),
        out_specs=(P("dp", "mp"), P("dp", "mp"), P("dp", "mp")),
        check_vma=False,
    )
```

profile of v0, /device:TPU:1, one launch (start us, length us, event | category | flops | bytes accessed | tf_op | source)
XLA Modules:
  0.0 296.0 jit_solution(5612822534412277168)
XLA Ops:
  8.0 0.0 copy-start
  8.0 0.0 reduce-scatter.2.cloned.1.call-start
  8.1 1.5 copy-done
  9.6 3.8 %fusion.6 = f32[512,512]{1,0:T(8,128)} fusion(bf16[512,2048]{1,0:T(8,128)(2,1)S(1)} %copy-done, bf16[2048,512]{1,0:T(8,128)(2,1)} %param.7), kind=kOutput, calls=%fused_computation.9 | convolution fusion | flops 1073741824 | bytes 5242880 | tf_op jit(solution)/shard_map/dot_general | solution.py:19
  13.4 28.0 %all-reduce.1 = bf16[512,512]{1,0:T(8,128)(2,1)S(1)} all-reduce(f32[512,512]{1,0:T(8,128)} %fusion.6), channel_id=1, replica_groups=mesh['dp'=64,'mp'=4] {'mp'}, use_global_device_ids=true, to_apply=%region_0.0 | all-reduce | flops 262144 | bytes 1572864 | tf_op jit(solution)/shard_map/psum | solution.py:20
  41.4 7.1 %fusion.7 = f32[512,3584]{1,0:T(8,128)} fusion(bf16[512,512]{1,0:T(8,128)(2,1)S(1)} %all-reduce.1, bf16[512,3584]{1,0:T(8,128)(2,1)} %param.6), kind=kOutput, calls=%fused_computation.10 | convolution fusion | flops 1879048192 | bytes 11534336 | tf_op jit(solution)/shard_map/dot_general | solution.py:22
  48.5 0.0 copy-start.1
  48.5 0.0 copy-start.2
  48.5 0.0 reduce-scatter.2.cloned.1.call-update
  48.5 0.0 all-gather.3.cloned.1.call-start
  48.6 0.5 all-gather.3.cloned.1.call-update
  49.1 0.0 all-gather.5.cloned.1.call-start
  49.2 151.1 %reduce-scatter.2.cloned.1.call-done = f32[8,3584]{1,0:T(8,128)} async-done(((f32[512,3584]{1,0:T(8,128)}), f32[8,3584]{1,0:T(8,128)}) %reduce-scatter.2.cloned.1.call-update) | async-done | bytes 114704 | tf_op jit(solution)/shard_map/reduce_scatter | solution.py:21
  200.2 0.0 copy-done.1
  200.2 0.0 copy-done.2
  200.2 1.6 divide_convert_fusion
  201.9 0.0 all-gather.5.cloned.1.call-update
  201.9 0.0 all-gather.3.cloned.1.call-done
  201.9 82.7 %all-gather.5.cloned.1.call-done = bf16[512,3584]{1,0:T(8,128)(2,1)} async-done(((bf16[8,3584]{1,0:T(8,128)(2,1)}), bf16[512,3584]{1,0:T(8,128)(2,1)}) %all-gather.5.cloned.1.call-update) | async-done | bytes 3670032 | tf_op jit(solution)/shard_map/all_gather | solution.py:37
  284.6 4.0 %convolution_multiply_fusion = f32[128,3584]{1,0:T(8,128)} fusion(bf16[512,3584]{1,0:T(8,128)(2,1)} %all-gather.5.cloned.1.call-done, bf16[8192,512]{1,0:T(8,128)(2,1)} %all-gather.3.cloned.1.call-done, s32[]{:T(128)S(6)} %select_n.3), kind=kOutput, calls=%fused_computation | convolution fusion | flops 470220800 | bytes 5636100 | tf_op jit(solution)/shard_map/dot_general | solution.py:35
Async XLA Ops:
  8.0 1.6 copy-start
  8.0 192.2 %reduce-scatter.2.cloned.1.call-start = ((), (), s32[]{:S(2)}) async-start(), calls=%async_computation.2 | async-start | bytes 7454720 | tf_op jit(solution)/shard_map/reduce_scatter | solution.py:21
  48.5 151.7 %copy-start.1 = (f32[8,3584]{1,0:T(8,128)S(1)}, f32[8,3584]{1,0:T(8,128)}, u32[]{:S(2)}) copy-start(f32[8,3584]{1,0:T(8,128)} %param.8) | copy-start | bytes 344068
  48.5 151.7 %copy-start.2 = (f32[8,3584]{1,0:T(8,128)S(1)}, f32[8,3584]{1,0:T(8,128)}, u32[]{:S(2)}) copy-start(f32[8,3584]{1,0:T(8,128)} %param.9) | copy-start | bytes 344068
  48.5 153.4 %all-gather.3.cloned.1.call-start = ((), (), s32[]{:S(2)}) async-start(), calls=%async_computation.1 | async-start | bytes 10485760 | tf_op jit(solution)/shard_map/all_gather | solution.py:33
  49.1 235.5 %all-gather.5.cloned.1.call-start = ((), (), s32[]{:S(2)}) async-start(), calls=%async_computation.3 | async-start | bytes 3727360 | tf_op jit(solution)/shard_map/all_gather | solution.py:37
Sparse Core Ops, SparseCore 0:
  48.7 151.5 reduce-scatter.1
Sparse Core Ops, SparseCore 1:
  50.8 92.2 all-gather.2
  202.0 82.6 all-gather.4
where the time goes:
time: 296 us
  waiting for transfers between devices  234 us (79%)
  blocking collectives  28 us (9%)
  between operations  15.5 us (5%)
  matrix products  14.9 us (5%)
    reduce_scatter x1, waiting for transfers between devices, body(): lax.psum_scatter(lax.dot_general(coeffs, up_cotangent, (((0,), (0,)), (()...  151 us
    all_gather x1, waiting for transfers between devices, body(): lax.all_gather(direction, 'dp', axis=0, tiled=True)  82.7 us
    psum x1, blocking collectives, body(): coeffs = lax.psum(partial_coeffs, 'mp').astype(jnp.bfloat16)  28 us
    dot_general x1, matrix products, body(): lax.dot_general(coeffs, up_cotangent, (((0,), (0,)), ((), ())), preferred...  7.14 us
  transfers between devices with their start and end apart: 3, of which 2 were waited for; matrix products, arithmetic and copies ran while one was open for 1% of the time, Pallas kernels for 0%

commit v1 on v0

v1 whole, which is shorter than its diff:
```python
import jax
import jax.numpy as jnp
from jax import lax
from jax.experimental import pallas as pl
from jax.experimental.pallas import tpu as pltpu
from jax.sharding import PartitionSpec as P

STEP = 10
NX, NY, NZ = 4, 4, 8
COLS = 3584
WIDTHS = (512, 512, 512, 512, 512, 512, 512)
STARTS = tuple(sum(WIDTHS[:i]) for i in range(len(WIDTHS)))
NCH = len(WIDTHS)
WMAX = max(WIDTHS)
KB = 4
F32, BF16 = jnp.float32, jnp.bfloat16


def adam_rows(first_moment, second_moment, low_grad):
    new_first = 0.9 * first_moment + 0.1 * low_grad
    new_second = 0.999 * second_moment + 0.001 * low_grad * low_grad
    first_hat = new_first / (1.0 - 0.9**STEP)
    second_hat = new_second / (1.0 - 0.999**STEP)
    direction = first_hat / (jnp.sqrt(second_hat) + 1e-08)
    return (new_first, new_second, direction)


def kernel(
    f_hbm, u_hbm, b_hbm, m_hbm, v_hbm,
    w_hbm, nm_hbm, nv_hbm,
    fv, bv, u, mv, vv, nm, nv,
    acc, pt, xs, xr, qv, ct,
    lf, ys, yr, zf, zs, zr, db, br, be, wo,
    ld_f, ld_b, ld_u, ld_m, st_o, st_m,
    sx, rx, sq, rq, su, ru, sb, rb,
    sy, ry, sz, rz, sg, rg, sh, rh, sk, rk,
):
    dp = lax.axis_index("dp")
    x = lax.axis_index("mp")
    c = lax.rem(dp, 2)
    z = lax.rem(dp // 2, NZ)
    y = dp // (2 * NZ)
    oc = 1 - c

    def dev(x_, y_, z_, c_):
        return ((y_ * NZ + z_) * 2 + c_, x_)

    def send(src, dst, ss, rs, to):
        return pltpu.make_async_remote_copy(
            src_ref=src, dst_ref=dst, send_sem=ss, recv_sem=rs,
            device_id=to, device_id_type=pl.DeviceIdType.MESH,
        )

    xd = [lax.rem(x + d, NX) for d in range(NX)]
    yd = [lax.rem(y + d, NY) for d in range(NY)]
    zd = [lax.rem(z + d, NZ) for d in range(NZ)]
    sib = dev(x, y, z, oc)

    kw = fv.shape[2]
    lf_c = [pltpu.make_async_copy(f_hbm.at[:, pl.ds(k * kw, kw)], fv.at[k], ld_f.at[k]) for k in range(KB)]
    lb_c = [pltpu.make_async_copy(b_hbm.at[pl.ds(k * kw, kw), :], bv.at[k], ld_b.at[k]) for k in range(KB)]
    for k in range(KB):
        lb_c[k].start()
        lf_c[k].start()
    lu = pltpu.make_async_copy(u_hbm, u.at[c], ld_u)
    lu.start()
    lm = pltpu.make_async_copy(m_hbm, mv, ld_m.at[0])
    lv = pltpu.make_async_copy(v_hbm, vv, ld_m.at[1])
    lm.start()
    lv.start()

    bar = pltpu.get_barrier_semaphore()
    peers = [sib]
    for d in range(1, NX):
        peers += [dev(xd[d], y, z, c), dev(xd[d], y, z, oc)]
    peers += [dev(x, yd[d], z, c) for d in range(1, NY)]
    peers += [dev(x, y, zd[d], c) for d in range(1, NZ)]
    for p in peers:
        pl.semaphore_signal(bar, inc=1, device_id=p, device_id_type=pl.DeviceIdType.MESH)

    for k in range(KB):
        lb_c[k].wait()
        lf_c[k].wait()
        part = jnp.dot(fv[k], bv[k], preferred_element_type=F32)
        if k == 0:
            acc[...] = part
        else:
            acc[...] += part
    for yy in range(NY):
        tt = acc[:, yy * 128:(yy + 1) * 128].T
        for h in range(2):
            for zl in range(4):
                for cc in range(2):
                    r = ((h * 4 + zl) * 2 + cc) * 8
                    pt[2 * cc + h, yy * 32 + zl * 8:yy * 32 + zl * 8 + 8, :] = tt[r:r + 8, :]
    xs[...] = pt[...].astype(BF16)

    pl.semaphore_wait(bar, len(peers))
    cx = [send(xs.at[xd[d]], xr.at[d - 1], sx.at[d - 1], rx.at[d - 1], dev(xd[d], y, z, c)) for d in range(1, NX)]
    for cp in cx:
        cp.start()
    cu = send(u_hbm, u.at[c], su, ru, sib)
    cu.start()
    cu_in = send(u_hbm, u.at[oc], su, ru, sib)

    for cp in cx:
        cp.wait_recv()
    q = pt[x]
    for d in range(NX - 1):
        q = q + xr[d].astype(F32)
    hx = lax.rem(x, 2)
    cq = x // 2
    qv[...] = q.astype(BF16)
    cqs = [send(qv, ct.at[c, hx], sq.at[d], rq.at[c, hx], dev(xd[d], y, z, cq)) for d in range(NX)]
    for d in range(1, NX):
        cqs[d].start()

    @pl.when(cq != c)
    def _():
        cqs[0].start()

    @pl.when(cq == c)
    def _():
        ct[c, hx] = qv[...]

    rows = br.shape[0]
    brow = lax.rem(dp, 16)
    src_b = bv.at[brow // 4, pl.ds(pl.multiple_of(lax.rem(brow, 4) * rows, rows), rows), :]
    cbs = [send(src_b, br, sb.at[d - 1], rb, dev(xd[d], y, z, c)) for d in range(1, NX)]

    @pl.when(x == y)
    def _():
        for cp in cbs:
            cp.start()
        loc = pltpu.make_async_copy(src_b, br, rb)
        loc.start()
        loc.wait()

    @pl.when(x != y)
    def _():
        cbs[0].wait_recv()

    ri = lax.broadcasted_iota(jnp.int32, (512, 512), 0)
    ji = lax.broadcasted_iota(jnp.int32, (512, 512), 1)
    jl = lax.broadcasted_iota(jnp.int32, (rows, 512), 1)
    for cc in range(2):
        e = (ri == (ji & ~8) + cc * 8).astype(F32).astype(BF16)
        t = jnp.dot(br[...], e, preferred_element_type=F32)
        for s in range(2):
            be[s, :, cc * 512:(cc + 1) * 512] = jnp.where(((jl >> 3) & 1) == s, t, 0.0).astype(BF16)

    for cc in range(2):
        for h in range(2):
            own = (2 * c + h == x) & (c == cc)
            cp = send(ct.at[cc, h], ct.at[cc, h], sq.at[0], rq.at[cc, h], sib)

            @pl.when(jnp.logical_not(own))
            def _():
                cp.wait_recv()
    lu.wait()
    cu_in.wait_recv()
    lm.wait()
    lv.wait()

    def y_copies(k):
        w = WIDTHS[k]
        return [
            send(ys.at[k, yd[d], :, pl.ds(0, w)], yr.at[k, d - 1, :, pl.ds(0, w)], sy.at[k, d - 1], ry.at[k, d - 1], dev(x, yd[d], z, c))
            for d in range(1, NY)
        ]

    def z_copies(k):
        w = WIDTHS[k] // 2
        return [
            send(zs.at[k, zd[d], :, pl.ds(0, w)], zr.at[k, d - 1, :, pl.ds(0, w)], sz.at[k, d - 1], rz.at[k, d - 1], dev(x, y, zd[d], c))
            for d in range(1, NZ)
        ]

    def gz_copies(k):
        w = WIDTHS[k] // 2
        mine = db.at[k, c, y, z, :, pl.ds(0, w)]
        out = [send(mine, mine, sg.at[k, d - 1], rg.at[k, d - 1], dev(x, y, zd[d], c)) for d in range(1, NZ)]
        inn = []
        for d in range(1, NZ):
            zz = lax.rem(z + NZ - d, NZ)
            theirs = db.at[k, c, y, zz, :, pl.ds(0, w)]
            inn.append(send(theirs, theirs, sg.at[k, d - 1], rg.at[k, d - 1], dev(x, y, zz, c)))
        return out, inn

    def gy_copies(k):
        w = WIDTHS[k] // 2
        blk = lambda yy: db.at[k, c, yy, :, :, pl.ds(0, w)]
        lo = lambda yy: db.at[k, c, yy, pl.ds(0, 4), :, pl.ds(0, w)]
        hi = lambda yy: db.at[k, c, yy, pl.ds(4, 4), :, pl.ds(0, w)]
        up, dn = dev(x, yd[1], z, c), dev(x, yd[3], z, c)
        first = [
            send(blk(y), blk(y), sh.at[k, 0], rh.at[k, 0], up),
            send(blk(y), blk(y), sh.at[k, 1], rh.at[k, 1], dn),
        ]
        first_in = [
            send(blk(yd[3]), blk(yd[3]), sh.at[k, 0], rh.at[k, 0], up),
            send(blk(yd[1]), blk(yd[1]), sh.at[k, 1], rh.at[k, 1], dn),
        ]
        second = [
            send(lo(yd[3]), lo(yd[3]), sh.at[k, 2], rh.at[k, 2], up),
            send(hi(yd[1]), hi(yd[1]), sh.at[k, 3], rh.at[k, 3], dn),
        ]
        second_in = [
            send(lo(yd[2]), lo(yd[2]), sh.at[k, 2], rh.at[k, 2], up),
            send(hi(yd[2]), hi(yd[2]), sh.at[k, 3], rh.at[k, 3], dn),
        ]
        return first, first_in, second, second_in

    def k_copies(k):
        w = WIDTHS[k] // 2
        blk = lambda cc, yy: db.at[k, cc, yy, :, :, pl.ds(0, w)]
        out = [send(blk(c, yd[d]), blk(c, yd[d]), sk.at[k, d], rk.at[k, d], sib) for d in range(NY)]
        inn = [send(blk(oc, yd[d]), blk(oc, yd[d]), sk.at[k, d], rk.at[k, d], sib) for d in range(NY)]
        return out, inn

    def out_copy(k):
        sl = pl.ds(STARTS[k], WIDTHS[k])
        return pltpu.make_async_copy(wo.at[:, sl], w_hbm.at[:, sl], st_o.at[k])

    def s1(k):
        s0, w = STARTS[k], WIDTHS[k]
        for h in range(2):
            l = jnp.dot(ct[0, h], u[0, :, s0:s0 + w], preferred_element_type=F32)
            l += jnp.dot(ct[1, h], u[1, :, s0:s0 + w], preferred_element_type=F32)
            for yy in range(NY):
                part = l[yy * 32:(yy + 1) * 32]
                lf[yy, h * 32:(h + 1) * 32, s0:s0 + w] = part
                ys[k, yy, h * 32:(h + 1) * 32, 0:w] = part.astype(BF16)
        for cp in y_copies(k):
            cp.start()

    def s2(k):
        s0, w = STARTS[k], WIDTHS[k]
        for cp in y_copies(k):
            cp.wait_recv()
        g = lf[y, :, s0:s0 + w]
        for d in range(NY - 1):
            g = g + yr[k, d, :, 0:w].astype(F32)
        for zz in range(NZ):
            part = g[zz * 8:(zz + 1) * 8]
            zf[zz, :, s0:s0 + w] = part
            zs[k, zz, :, 0:w // 2] = jnp.concatenate([part[:, :w // 2], part[:, w // 2:]], axis=0).astype(BF16)
        for cp in z_copies(k):
            cp.start()

    def s3(k):
        s0, w = STARTS[k], WIDTHS[k]
        for cp in z_copies(k):
            cp.wait_recv()
        t = zr[k, 0, :, 0:w // 2].astype(F32)
        for d in range(1, NZ - 1):
            t = t + zr[k, d, :, 0:w // 2].astype(F32)
        g = zf[z, :, s0:s0 + w] + jnp.concatenate([t[0:8], t[8:16]], axis=1)
        a, b, dr = adam_rows(mv[:, s0:s0 + w], vv[:, s0:s0 + w], g)
        nm[:, s0:s0 + w] = a
        nv[:, s0:s0 + w] = b
        db[k, c, y, z, :, 0:w // 2] = jnp.concatenate([dr[:, :w // 2], dr[:, w // 2:]], axis=0).astype(BF16)
        for cp in gz_copies(k)[0]:
            cp.start()

    def s4(k):
        for cp in gz_copies(k)[1]:
            cp.wait_recv()
        for cp in gy_copies(k)[0]:
            cp.start()
        k_copies(k)[0][0].start()

    def s5(k):
        _, first_in, second, _ = gy_copies(k)
        out = k_copies(k)[0]
        first_in[0].wait_recv()
        second[0].start()
        first_in[1].wait_recv()
        second[1].start()
        out[3].start()
        out[1].start()

    def s6(k):
        for cp in gy_copies(k)[3]:
            cp.wait_recv()
        k_copies(k)[0][2].start()

    def s7(k):
        s0, w = STARTS[k], WIDTHS[k]
        for cp in k_copies(k)[1]:
            cp.wait_recv()
        d_all = db[k, :, :, :, :, 0:w // 2].reshape(1024, w // 2)
        for s in range(2):
            o = s0 + s * (w // 2)
            wo[:, o:o + w // 2] = 0.25 * jnp.dot(be[s], d_all, preferred_element_type=F32)
        out_copy(k).start()

    om = [pltpu.make_async_copy(nm, nm_hbm, st_m.at[0]), pltpu.make_async_copy(nv, nv_hbm, st_m.at[1])]
    stages = [s1, s2, s3, s4, s5, s6, s7]
    for k in range(NCH):
        s1(k)
    for t in range(NCH + len(stages) - 2):
        for i in range(len(stages) - 1, 0, -1):
            k = t - (i - 1)
            if 0 <= k < NCH:
                stages[i](k)
                if i == 2 and k == NCH - 1:
                    om[0].start()
                    om[1].start()

    for cp in cx:
        cp.wait_send()
    cu.wait_send()
    for d in range(1, NX):
        cqs[d].wait_send()

    @pl.when(cq != c)
    def _():
        cqs[0].wait_send()

    @pl.when(x == y)
    def _():
        for cp in cbs:
            cp.wait_send()

    for k in range(NCH):
        first, _, second, _ = gy_copies(k)
        for cp in y_copies(k) + z_copies(k) + gz_copies(k)[0] + first + second + k_copies(k)[0]:
            cp.wait_send()
        out_copy(k).wait()
    om[0].wait()
    om[1].wait()


def body(features, up_cotangent, proj_basis, first_moment, second_moment):
    tok, feat = features.shape
    depth, rank = proj_basis.shape
    cols = up_cotangent.shape[1]
    kw = feat // KB
    rows = 128
    dma = pltpu.SemaphoreType.DMA
    anyspec = pl.BlockSpec(memory_space=pl.ANY)
    wu, nf, ns = pl.pallas_call(
        kernel,
        out_shape=(
            jax.ShapeDtypeStruct((rows, cols), F32),
            jax.ShapeDtypeStruct(first_moment.shape, F32),
            jax.ShapeDtypeStruct(second_moment.shape, F32),
        ),
        in_specs=[anyspec] * 5,
        out_specs=(anyspec,) * 3,
        scratch_shapes=[
            pltpu.VMEM((KB, tok, kw), BF16),
            pltpu.VMEM((KB, kw, rank), BF16),
            pltpu.VMEM((2, tok, cols), BF16),
            pltpu.VMEM((8, cols), F32),
            pltpu.VMEM((8, cols), F32),
            pltpu.VMEM((8, cols), F32),
            pltpu.VMEM((8, cols), F32),
            pltpu.VMEM((tok, rank), F32),
            pltpu.VMEM((NX, 128, tok), F32),
            pltpu.VMEM((NX, 128, tok), BF16),
            pltpu.VMEM((NX - 1, 128, tok), BF16),
            pltpu.VMEM((128, tok), BF16),
            pltpu.VMEM((2, 2, 128, tok), BF16),
            pltpu.VMEM((NY, 64, cols), F32),
            pltpu.VMEM((NCH, NY, 64, WMAX), BF16),
            pltpu.VMEM((NCH, NY - 1, 64, WMAX), BF16),
            pltpu.VMEM((NZ, 8, cols), F32),
            pltpu.VMEM((NCH, NZ, 16, WMAX // 2), BF16),
            pltpu.VMEM((NCH, NZ - 1, 16, WMAX // 2), BF16),
            pltpu.VMEM((NCH, 2, NY, NZ, 16, WMAX // 2), BF16),
            pltpu.VMEM((rows, rank), BF16),
            pltpu.VMEM((2, rows, 2 * rank), BF16),
            pltpu.VMEM((rows, cols), F32),
            dma((KB,)), dma((KB,)), dma(()), dma((2,)), dma((NCH,)), dma((2,)),
            dma((3,)), dma((3,)), dma((4,)), dma((2, 2)), dma(()), dma(()), dma((3,)), dma(()),
            dma((NCH, 3)), dma((NCH, 3)), dma((NCH, 7)), dma((NCH, 7)), dma((NCH, 7)), dma((NCH, 7)),
            dma((NCH, 4)), dma((NCH, 4)), dma((NCH, 4)), dma((NCH, 4)),
        ],
        compiler_params=pltpu.CompilerParams(
            collective_id=0, has_side_effects=True, vmem_limit_bytes=56 * 2**20
        ),
        cost_estimate=pl.CostEstimate(flops=4 * 10**9, bytes_accessed=12 * 10**6, transcendentals=0),
        name="galore",
    )(features, up_cotangent, proj_basis, first_moment, second_moment)
    return (wu, nf, ns)


def solution(mesh):
    return jax.shard_map(
        body,
        mesh=mesh,
        in_specs=(P("dp", "mp"), P("dp", "mp"), P("mp", None), P("dp", "mp"), P("dp", "mp")),
        out_specs=(P("dp", "mp"), P("dp", "mp"), P("dp", "mp")),
        check_vma=False,
    )
```

time: 296 us -> 102 us (0.34)
  waiting for transfers between devices: 234 us -> 0 us
  Pallas kernels: 0 us -> 97.5 us
  blocking collectives: 28 us -> 0 us
  matrix products: 14.9 us -> 0 us
  between operations: 15.5 us -> 0.66 us
    reduce_scatter x1 -> x0, waiting for transfers between devices: 151 us -> none  [body(): lax.psum_scatter(lax.dot_general(coeffs, up_cotangent, (((0,), (0,)), (()...]
    pallas_call x0 -> x1, Pallas kernels: none -> 97.5 us  [body(): pl.pallas_call(kernel, out_shape=(jax.ShapeDtypeStruct((rows, cols), F32)...]
    all_gather x2 -> x0, waiting for transfers between devices: 82.7 us -> none  [the longest x1 82.7 us: body(): lax.all_gather(direction, 'dp', axis=0, tiled=True)]
    psum x1 -> x0, blocking collectives: 28 us -> none  [body(): coeffs = lax.psum(partial_coeffs, 'mp').astype(jnp.bfloat16)]
    dot_general x3 -> x0, matrix products: 14.9 us -> none  [the longest x1 7.14 us: body(): lax.dot_general(coeffs, up_cotangent, (((0,), (0,)), ((), ())), preferred...]
  transfers between devices with their start and end apart: 3 -> 0, of which waited for: 2 -> 0; matrix products, arithmetic and copies ran while one was open for 1% -> 0% of each run, Pallas kernels for 0% -> 0%
where the time goes in v1:
time: 102 us
  Pallas kernels  97.5 us (96%)
  local copies, waits for them, and re-layouts  4.2 us (4%)
    pallas_call x1, Pallas kernels, body(): pl.pallas_call(kernel, out_shape=(jax.ShapeDtypeStruct((rows, cols), F32)...  97.5 us
    unnamed x7, local copies, waits for them, and re-layouts  4.2 us

profile of v1, /device:TPU:1, one launch (start us, length us, event | category | flops | bytes accessed | tf_op | source)
XLA Modules:
  0.0 102.4 jit_solution(10380448589250023376)
XLA Ops:
  0.6 97.5 %galore.1 = (f32[128,3584]{1,0:T(8,128)}, f32[8,3584]{1,0:T(8,128)}, f32[8,3584]{1,0:T(8,128)}) custom-call(bf16[512,2048]{1,0:T(8,128)(2,1)} %f_hbm.1, bf16[512,3584]{1,0:T(8,128)(2,1)} %u_hbm.1, bf16[2048,512]{1,0:T(8,128)(2,1)} %b_hbm.1, f32[8,3584]{1,0:T(8,128)} %m_hbm.1, f32[8,3584]{1,0:T(8,128)} %v_hbm.1), custom_call_target="tpu_custom_call" | custom-call | flops 4000000000 | bytes 12000000 | tf_op jit(solution)/shard_map/galore/pallas_call | solution.py:343
  98.2 0.0 copy-start.1
  98.2 0.0 copy-start
  98.2 2.9 %copy.11 = f32[128,3584]{1,0:T(8,128)} copy(f32[128,3584]{1,0:T(8,128)} %get-tuple-element.6) | data formatting | bytes 3670016
  101.1 0.0 copy-done.1
  101.1 0.6 copy.12
  101.7 0.0 copy-done
  101.7 0.6 copy.13
Async XLA Ops:
  98.2 2.9 %copy-start.1 = (f32[8,3584]{1,0:T(8,128)S(1)}, f32[8,3584]{1,0:T(8,128)}, u32[]{:S(2)}) copy-start(f32[8,3584]{1,0:T(8,128)} %get-tuple-element.7) | copy-start | bytes 344068
  98.2 3.6 %copy-start = (f32[8,3584]{1,0:T(8,128)S(1)}, f32[8,3584]{1,0:T(8,128)}, u32[]{:S(2)}) copy-start(f32[8,3584]{1,0:T(8,128)} %get-tuple-element.8) | copy-start | bytes 344068

commit v2 on v1

--- a/solution.py
+++ b/solution.py
@@ -6,6 +6,9 @@
 from jax.sharding import PartitionSpec as P
 
 STEP = 10
+PACE = 1.3
+LATENCY = (3.5, 5.5, 5.5, 4.0, 4.0, 2.0, 0.0)
+PARTS = (pl.ds(0, 1), pl.ds(1, 3))
 NX, NY, NZ = 4, 4, 8
 COLS = 3584
 WIDTHS = (512, 512, 512, 512, 512, 512, 512)
@@ -27,11 +30,11 @@
 
 def kernel(
     f_hbm, u_hbm, b_hbm, m_hbm, v_hbm,
-    w_hbm, nm_hbm, nv_hbm,
-    fv, bv, u, mv, vv, nm, nv,
+    wo, nm, nv,
+    fv, bv, u, mv, vv,
     acc, pt, xs, xr, qv, ct,
-    lf, ys, yr, zf, zs, zr, db, br, be, wo,
-    ld_f, ld_b, ld_u, ld_m, st_o, st_m,
+    lf, ys, yr, zf, zs, zr, db, br, be,
+    ld_f, ld_b, ld_u, ld_m,
     sx, rx, sq, rq, su, ru, sb, rb,
     sy, ry, sz, rz, sg, rg, sh, rh, sk, rk,
 ):
@@ -54,6 +57,7 @@
     xd = [lax.rem(x + d, NX) for d in range(NX)]
     yd = [lax.rem(y + d, NY) for d in range(NY)]
     zd = [lax.rem(z + d, NZ) for d in range(NZ)]
+    yo = [yd[2], yd[1], yd[3], yd[0]]
     sib = dev(x, y, z, oc)
 
     kw = fv.shape[2]
@@ -92,82 +96,100 @@
             for zl in range(4):
                 for cc in range(2):
                     r = ((h * 4 + zl) * 2 + cc) * 8
-                    pt[2 * cc + h, yy * 32 + zl * 8:yy * 32 + zl * 8 + 8, :] = tt[r:r + 8, :]
-    xs[...] = pt[...].astype(BF16)
+                    pt[2 * cc + h, yy, zl * 8:zl * 8 + 8, :] = tt[r:r + 8, :]
+    for j in range(NY):
+        for xx in range(NX):
+            xs[xx, j] = pt[xx, yo[j]].astype(BF16)
 
     pl.semaphore_wait(bar, len(peers))
-    cx = [send(xs.at[xd[d]], xr.at[d - 1], sx.at[d - 1], rx.at[d - 1], dev(xd[d], y, z, c)) for d in range(1, NX)]
-    for cp in cx:
-        cp.start()
+    cx = [
+        [
+            send(xs.at[xd[d], sl], xr.at[d - 1, sl], sx.at[p, d - 1], rx.at[p, d - 1], dev(xd[d], y, z, c))
+            for d in range(1, NX)
+        ]
+        for p, sl in enumerate(PARTS)
+    ]
+    for p in range(2):
+        for cp in cx[p]:
+            cp.start()
     cu = send(u_hbm, u.at[c], su, ru, sib)
     cu.start()
     cu_in = send(u_hbm, u.at[oc], su, ru, sib)
 
-    for cp in cx:
-        cp.wait_recv()
-    q = pt[x]
-    for d in range(NX - 1):
-        q = q + xr[d].astype(F32)
     hx = lax.rem(x, 2)
     cq = x // 2
-    qv[...] = q.astype(BF16)
-    cqs = [send(qv, ct.at[c, hx], sq.at[d], rq.at[c, hx], dev(xd[d], y, z, cq)) for d in range(NX)]
-    for d in range(1, NX):
-        cqs[d].start()
-
-    @pl.when(cq != c)
-    def _():
-        cqs[0].start()
-
-    @pl.when(cq == c)
-    def _():
-        ct[c, hx] = qv[...]
+
+    def q_copies(p):
+        sl = PARTS[p]
+        return [send(qv.at[sl], ct.at[c, hx, sl], sq.at[p, d], rq.at[p, c, hx], dev(xd[d], y, z, cq)) for d in range(NX)]
+
+    def x_reduce(p):
+        for cp in cx[p]:
+            cp.wait_recv()
+        for j in (0,) if p == 0 else (1, 2, 3):
+            q = pt[x, yo[j]]
+            for d in range(NX - 1):
+                q = q + xr[d, j].astype(F32)
+            qv[j] = q.astype(BF16)
+        cps = q_copies(p)
+        for d in range(1, NX):
+            cps[d].start()
+
+        @pl.when(cq != c)
+        def _():
+            cps[0].start()
+
+        @pl.when(cq == c)
+        def _():
+            for j in (0,) if p == 0 else (1, 2, 3):
+                ct[c, hx, j] = qv[j]
+
+    def x_gathered(p):
+        sl = PARTS[p]
+        for cc in range(2):
+            for h in range(2):
+                own = (2 * c + h == x) & (c == cc)
+
+                @pl.when(jnp.logical_not(own))
+                def _():
+                    send(ct.at[cc, h, sl], ct.at[cc, h, sl], sq.at[p, 0], rq.at[p, cc, h], sib).wait_recv()
 
     rows = br.shape[0]
     brow = lax.rem(dp, 16)
     src_b = bv.at[brow // 4, pl.ds(pl.multiple_of(lax.rem(brow, 4) * rows, rows), rows), :]
     cbs = [send(src_b, br, sb.at[d - 1], rb, dev(xd[d], y, z, c)) for d in range(1, NX)]
 
-    @pl.when(x == y)
-    def _():
-        for cp in cbs:
-            cp.start()
-        loc = pltpu.make_async_copy(src_b, br, rb)
-        loc.start()
-        loc.wait()
-
-    @pl.when(x != y)
-    def _():
-        cbs[0].wait_recv()
-
-    ri = lax.broadcasted_iota(jnp.int32, (512, 512), 0)
-    ji = lax.broadcasted_iota(jnp.int32, (512, 512), 1)
-    jl = lax.broadcasted_iota(jnp.int32, (rows, 512), 1)
-    for cc in range(2):
-        e = (ri == (ji & ~8) + cc * 8).astype(F32).astype(BF16)
-        t = jnp.dot(br[...], e, preferred_element_type=F32)
-        for s in range(2):
-            be[s, :, cc * 512:(cc + 1) * 512] = jnp.where(((jl >> 3) & 1) == s, t, 0.0).astype(BF16)
-
-    for cc in range(2):
-        for h in range(2):
-            own = (2 * c + h == x) & (c == cc)
-            cp = send(ct.at[cc, h], ct.at[cc, h], sq.at[0], rq.at[cc, h], sib)
-
-            @pl.when(jnp.logical_not(own))
-            def _():
-                cp.wait_recv()
-    lu.wait()
-    cu_in.wait_recv()
-    lm.wait()
-    lv.wait()
+    def basis_send():
+        @pl.when(x == y)
+        def _():
+            for cp in cbs:
+                cp.start()
+
+    def basis_columns():
+        @pl.when(x == y)
+        def _():
+            loc = pltpu.make_async_copy(src_b, br, rb)
+            loc.start()
+            loc.wait()
+
+        @pl.when(x != y)
+        def _():
+            cbs[0].wait_recv()
+
+        ri = lax.broadcasted_iota(jnp.int32, (512, 512), 0)
+        ji = lax.broadcasted_iota(jnp.int32, (512, 512), 1)
+        jl = lax.broadcasted_iota(jnp.int32, (rows, 512), 1)
+        for cc in range(2):
+            e = (ri == (ji & ~8) + cc * 8).astype(F32).astype(BF16)
+            t = jnp.dot(br[...], e, preferred_element_type=F32)
+            for s in range(2):
+                be[s, :, cc * 512:(cc + 1) * 512] = jnp.where(((jl >> 3) & 1) == s, t, 0.0).astype(BF16)
 
     def y_copies(k):
-        w = WIDTHS[k]
-        return [
-            send(ys.at[k, yd[d], :, pl.ds(0, w)], yr.at[k, d - 1, :, pl.ds(0, w)], sy.at[k, d - 1], ry.at[k, d - 1], dev(x, yd[d], z, c))
-            for d in range(1, NY)
-        ]
+        w = pl.ds(0, WIDTHS[k])
+        up, dn = dev(x, yd[1], z, c), dev(x, yd[3], z, c)
+        to = (up, up, dn) if k % 2 == 0 else (dn, dn, up)
+        return [send(ys.at[k, i, :, w], yr.at[k, i, :, w], sy.at[k, i], ry.at[k, i], to[i]) for i in range(3)]
 
     def z_copies(k):
         w = WIDTHS[k] // 2
@@ -218,29 +240,39 @@
         inn = [send(blk(oc, yd[d]), blk(oc, yd[d]), sk.at[k, d], rk.at[k, d], sib) for d in range(NY)]
         return out, inn
 
-    def out_copy(k):
-        sl = pl.ds(STARTS[k], WIDTHS[k])
-        return pltpu.make_async_copy(wo.at[:, sl], w_hbm.at[:, sl], st_o.at[k])
+    def low(j0, j1, k):
+        s0, w = STARTS[k], WIDTHS[k]
+        n = (j1 - j0) * 32
+        parts = []
+        for h in range(2):
+            l = jnp.dot(ct[0, h, j0:j1].reshape(n, -1), u[0, :, s0:s0 + w], preferred_element_type=F32)
+            l += jnp.dot(ct[1, h, j0:j1].reshape(n, -1), u[1, :, s0:s0 + w], preferred_element_type=F32)
+            parts.append(l)
+        return [jnp.concatenate([q[i * 32:(i + 1) * 32] for q in parts], axis=0) for i in range(j1 - j0)]
+
+    def s0(k):
+        w = WIDTHS[k]
+        ys[k, 0, :, 0:w] = low(0, 1, k)[0].astype(BF16)
+        y_copies(k)[0].start()
 
     def s1(k):
         s0, w = STARTS[k], WIDTHS[k]
-        for h in range(2):
-            l = jnp.dot(ct[0, h], u[0, :, s0:s0 + w], preferred_element_type=F32)
-            l += jnp.dot(ct[1, h], u[1, :, s0:s0 + w], preferred_element_type=F32)
-            for yy in range(NY):
-                part = l[yy * 32:(yy + 1) * 32]
-                lf[yy, h * 32:(h + 1) * 32, s0:s0 + w] = part
-                ys[k, yy, h * 32:(h + 1) * 32, 0:w] = part.astype(BF16)
-        for cp in y_copies(k):
-            cp.start()
+        up, dn, own = low(1, 4, k)
+        relayed, direct = (up, dn) if k % 2 == 0 else (dn, up)
+        lf[:, s0:s0 + w] = own
+        cps = y_copies(k)
+        ys[k, 2, :, 0:w] = direct.astype(BF16)
+        cps[2].start()
+        cps[0].wait_recv()
+        ys[k, 1, :, 0:w] = (relayed + yr[k, 0, :, 0:w].astype(F32)).astype(BF16)
+        cps[1].start()
 
     def s2(k):
         s0, w = STARTS[k], WIDTHS[k]
-        for cp in y_copies(k):
-            cp.wait_recv()
-        g = lf[y, :, s0:s0 + w]
-        for d in range(NY - 1):
-            g = g + yr[k, d, :, 0:w].astype(F32)
+        g = lf[:, s0:s0 + w]
+        for i in (2, 1):
+            y_copies(k)[i].wait_recv()
+            g = g + yr[k, i, :, 0:w].astype(F32)
         for zz in range(NZ):
             part = g[zz * 8:(zz + 1) * 8]
             zf[zz, :, s0:s0 + w] = part
@@ -293,30 +325,42 @@
         for s in range(2):
             o = s0 + s * (w // 2)
             wo[:, o:o + w // 2] = 0.25 * jnp.dot(be[s], d_all, preferred_element_type=F32)
-        out_copy(k).start()
-
-    om = [pltpu.make_async_copy(nm, nm_hbm, st_m.at[0]), pltpu.make_async_copy(nv, nv_hbm, st_m.at[1])]
+
+    x_reduce(0)
+    x_reduce(1)
+    lu.wait()
+    cu_in.wait_recv()
+    x_gathered(0)
+    for k in range(NCH):
+        s0(k)
+    x_gathered(1)
+    lm.wait()
+    lv.wait()
+    basis_send()
+
     stages = [s1, s2, s3, s4, s5, s6, s7]
+    order = []
     for k in range(NCH):
-        s1(k)
-    for t in range(NCH + len(stages) - 2):
-        for i in range(len(stages) - 1, 0, -1):
-            k = t - (i - 1)
-            if 0 <= k < NCH:
-                stages[i](k)
-                if i == 2 and k == NCH - 1:
-                    om[0].start()
-                    om[1].start()
-
-    for cp in cx:
-        cp.wait_send()
+        t = PACE * k
+        for i in range(len(stages)):
+            order.append((t, -i, k))
+            t += LATENCY[i]
+    for n, (_, i, k) in enumerate(sorted(order)):
+        stages[-i](k)
+        if i == -1 and k == NCH - 1:
+            basis_columns()
+
+    for p in range(2):
+        for cp in cx[p]:
+            cp.wait_send()
+        for d in range(1, NX):
+            q_copies(p)[d].wait_send()
+
+        @pl.when(cq != c)
+        def _():
+            q_copies(p)[0].wait_send()
+
     cu.wait_send()
-    for d in range(1, NX):
-        cqs[d].wait_send()
-
-    @pl.when(cq != c)
-    def _():
-        cqs[0].wait_send()
 
     @pl.when(x == y)
     def _():
@@ -327,9 +371,6 @@
         first, _, second, _ = gy_copies(k)
         for cp in y_copies(k) + z_copies(k) + gz_copies(k)[0] + first + second + k_copies(k)[0]:
             cp.wait_send()
-        out_copy(k).wait()
-    om[0].wait()
-    om[1].wait()
 
 
 def body(features, up_cotangent, proj_basis, first_moment, second_moment):
@@ -343,38 +384,35 @@
     wu, nf, ns = pl.pallas_call(
         kernel,
         out_shape=(
-            jax.ShapeDtypeStruct((rows, cols), F32),
-            jax.ShapeDtypeStruct(first_moment.shape, F32),
-            jax.ShapeDtypeStruct(second_moment.shape, F32),
+            pltpu.VMEM((rows, cols), F32),
+            pltpu.VMEM(first_moment.shape, F32),
+            pltpu.VMEM(second_moment.shape, F32),
         ),
         in_specs=[anyspec] * 5,
-        out_specs=(anyspec,) * 3,
+        out_specs=(pl.BlockSpec(memory_space=pltpu.VMEM),) * 3,
         scratch_shapes=[
             pltpu.VMEM((KB, tok, kw), BF16),
             pltpu.VMEM((KB, kw, rank), BF16),
             pltpu.VMEM((2, tok, cols), BF16),
             pltpu.VMEM((8, cols), F32),
             pltpu.VMEM((8, cols), F32),
-            pltpu.VMEM((8, cols), F32),
-            pltpu.VMEM((8, cols), F32),
             pltpu.VMEM((tok, rank), F32),
-            pltpu.VMEM((NX, 128, tok), F32),
-            pltpu.VMEM((NX, 128, tok), BF16),
-            pltpu.VMEM((NX - 1, 128, tok), BF16),
-            pltpu.VMEM((128, tok), BF16),
-            pltpu.VMEM((2, 2, 128, tok), BF16),
-            pltpu.VMEM((NY, 64, cols), F32),
-            pltpu.VMEM((NCH, NY, 64, WMAX), BF16),
-            pltpu.VMEM((NCH, NY - 1, 64, WMAX), BF16),
+            pltpu.VMEM((NX, NY, 32, tok), F32),
+            pltpu.VMEM((NX, NY, 32, tok), BF16),
+            pltpu.VMEM((NX - 1, NY, 32, tok), BF16),
+            pltpu.VMEM((NY, 32, tok), BF16),
+            pltpu.VMEM((2, 2, NY, 32, tok), BF16),
+            pltpu.VMEM((64, cols), F32),
+            pltpu.VMEM((NCH, 3, 64, WMAX), BF16),
+            pltpu.VMEM((NCH, 3, 64, WMAX), BF16),
             pltpu.VMEM((NZ, 8, cols), F32),
             pltpu.VMEM((NCH, NZ, 16, WMAX // 2), BF16),
             pltpu.VMEM((NCH, NZ - 1, 16, WMAX // 2), BF16),
             pltpu.VMEM((NCH, 2, NY, NZ, 16, WMAX // 2), BF16),
             pltpu.VMEM((rows, rank), BF16),
             pltpu.VMEM((2, rows, 2 * rank), BF16),
-            pltpu.VMEM((rows, cols), F32),
-            dma((KB,)), dma((KB,)), dma(()), dma((2,)), dma((NCH,)), dma((2,)),
-            dma((3,)), dma((3,)), dma((4,)), dma((2, 2)), dma(()), dma(()), dma((3,)), dma(()),
+            dma((KB,)), dma((KB,)), dma(()), dma((2,)),
+            dma((2, 3)), dma((2, 3)), dma((2, 4)), dma((2, 2, 2)), dma(()), dma(()), dma((3,)), dma(()),
             dma((NCH, 3)), dma((NCH, 3)), dma((NCH, 7)), dma((NCH, 7)), dma((NCH, 7)), dma((NCH, 7)),
             dma((NCH, 4)), dma((NCH, 4)), dma((NCH, 4)), dma((NCH, 4)),
         ],

time: 102 us -> 72.2 us (0.71)
  Pallas kernels: 97.5 us -> 69 us
  local copies, waits for them, and re-layouts: 4.2 us -> 2.52 us
    pallas_call x1, Pallas kernels: 97.5 us -> 69 us  [body(): pl.pallas_call(kernel, out_shape=(pltpu.VMEM((rows, cols), F32), pltpu.VM...]
    unnamed x7 -> x3, local copies, waits for them, and re-layouts: 4.2 us -> 2.52 us
where the time goes in v2:
time: 72.2 us; the launch traced here: 72.1 us
  Pallas kernels  69 us (96%)
  local copies, waits for them, and re-layouts  2.52 us (3%)
    pallas_call x1, Pallas kernels, body(): pl.pallas_call(kernel, out_shape=(pltpu.VMEM((rows, cols), F32), pltpu.VM...  69 us
    unnamed x3, local copies, waits for them, and re-layouts  2.52 us

profile of v2, /device:TPU:1, one launch (start us, length us, event | category | flops | bytes accessed | tf_op | source)
XLA Modules:
  0.0 72.1 jit_solution(1593131752824485202)
XLA Ops:
  0.6 69.0 %galore.1 = (f32[128,3584]{1,0:T(8,128)S(1)}, f32[8,3584]{1,0:T(8,128)S(1)}, f32[8,3584]{1,0:T(8,128)S(1)}) custom-call(bf16[512,2048]{1,0:T(8,128)(2,1)} %f_hbm.1, bf16[512,3584]{1,0:T(8,128)(2,1)} %u_hbm.1, bf16[2048,512]{1,0:T(8,128)(2,1)} %b_hbm.1, f32[8,3584]{1,0:T(8,128)} %m_hbm.1, f32[8,3584]{1,0:T(8,128)} %v_hbm.1), custom_call_target="tpu_custom_call" | custom-call | flops 4000000000 | bytes 12000000 | tf_op jit(solution)/shard_map/galore/pallas_call | solution.py:384
  69.6 1.2 %copy.11 = f32[128,3584]{1,0:T(8,128)} copy(f32[128,3584]{1,0:T(8,128)S(1)} %get-tuple-element.3) | data formatting | bytes 3670016
  70.8 0.6 copy.12
  71.5 0.6 copy.13

commit v3 on v2

--- a/solution.py
+++ b/solution.py
@@ -6,8 +6,9 @@
 from jax.sharding import PartitionSpec as P
 
 STEP = 10
-PACE = 1.3
-LATENCY = (3.5, 5.5, 5.5, 4.0, 4.0, 2.0, 0.0)
+P_START, P_PACE, Q_PACE, BASIS_AT = 0.1, 0.8, 5.0, 12.0
+P1, P2, P3, P4, P5, P6 = 3.5, 5.5, 5.5, 4.0, 4.0, 2.0
+Q1, Q2, Q3, Q4, Q5 = 9.0, 3.5, 3.5, 9.0, 2.0
 PARTS = (pl.ds(0, 1), pl.ds(1, 3))
 NX, NY, NZ = 4, 4, 8
 COLS = 3584
@@ -15,6 +16,7 @@
 STARTS = tuple(sum(WIDTHS[:i]) for i in range(len(WIDTHS)))
 NCH = len(WIDTHS)
 WMAX = max(WIDTHS)
+NQ = 1
 KB = 4
 F32, BF16 = jnp.float32, jnp.bfloat16
 
@@ -32,11 +34,12 @@
     f_hbm, u_hbm, b_hbm, m_hbm, v_hbm,
     wo, nm, nv,
     fv, bv, u, mv, vv,
-    acc, pt, xs, xr, qv, ct,
+    acc, pt, xs, xr, qv, ct, qs, qr, qf, qys, qyr,
     lf, ys, yr, zf, zs, zr, db, br, be,
     ld_f, ld_b, ld_u, ld_m,
     sx, rx, sq, rq, su, ru, sb, rb,
     sy, ry, sz, rz, sg, rg, sh, rh, sk, rk,
+    sqz, rqz, sqy, rqy, sqg, rqg, sqh, rqh,
 ):
     dp = lax.axis_index("dp")
     x = lax.axis_index("mp")
@@ -189,25 +192,20 @@
         w = pl.ds(0, WIDTHS[k])
         up, dn = dev(x, yd[1], z, c), dev(x, yd[3], z, c)
         to = (up, up, dn) if k % 2 == 0 else (dn, dn, up)
-        return [send(ys.at[k, i, :, w], yr.at[k, i, :, w], sy.at[k, i], ry.at[k, i], to[i]) for i in range(3)]
+        return [send(ys.at[k, i, :, w], yr.at[k, i, :, w], sy, ry.at[k, i], to[i]) for i in range(3)]
 
     def z_copies(k):
         w = WIDTHS[k] // 2
         return [
-            send(zs.at[k, zd[d], :, pl.ds(0, w)], zr.at[k, d - 1, :, pl.ds(0, w)], sz.at[k, d - 1], rz.at[k, d - 1], dev(x, y, zd[d], c))
+            send(zs.at[k, zd[d], :, pl.ds(0, w)], zr.at[k, d - 1, :, pl.ds(0, w)], sz, rz.at[k], dev(x, y, zd[d], c))
             for d in range(1, NZ)
         ]
 
     def gz_copies(k):
         w = WIDTHS[k] // 2
         mine = db.at[k, c, y, z, :, pl.ds(0, w)]
-        out = [send(mine, mine, sg.at[k, d - 1], rg.at[k, d - 1], dev(x, y, zd[d], c)) for d in range(1, NZ)]
-        inn = []
-        for d in range(1, NZ):
-            zz = lax.rem(z + NZ - d, NZ)
-            theirs = db.at[k, c, y, zz, :, pl.ds(0, w)]
-            inn.append(send(theirs, theirs, sg.at[k, d - 1], rg.at[k, d - 1], dev(x, y, zz, c)))
-        return out, inn
+        out = [send(mine, mine, sg, rg.at[k], dev(x, y, zd[d], c)) for d in range(1, NZ)]
+        return out
 
     def gy_copies(k):
         w = WIDTHS[k] // 2
@@ -216,29 +214,23 @@
         hi = lambda yy: db.at[k, c, yy, pl.ds(4, 4), :, pl.ds(0, w)]
         up, dn = dev(x, yd[1], z, c), dev(x, yd[3], z, c)
         first = [
-            send(blk(y), blk(y), sh.at[k, 0], rh.at[k, 0], up),
-            send(blk(y), blk(y), sh.at[k, 1], rh.at[k, 1], dn),
+            send(blk(y), blk(y), sh, rh.at[k, 0], up),
+            send(blk(y), blk(y), sh, rh.at[k, 1], dn),
         ]
         first_in = [
-            send(blk(yd[3]), blk(yd[3]), sh.at[k, 0], rh.at[k, 0], up),
-            send(blk(yd[1]), blk(yd[1]), sh.at[k, 1], rh.at[k, 1], dn),
+            send(blk(yd[3]), blk(yd[3]), sh, rh.at[k, 0], up),
+            send(blk(yd[1]), blk(yd[1]), sh, rh.at[k, 1], dn),
         ]
         second = [
-            send(lo(yd[3]), lo(yd[3]), sh.at[k, 2], rh.at[k, 2], up),
-            send(hi(yd[1]), hi(yd[1]), sh.at[k, 3], rh.at[k, 3], dn),
-        ]
-        second_in = [
-            send(lo(yd[2]), lo(yd[2]), sh.at[k, 2], rh.at[k, 2], up),
-            send(hi(yd[2]), hi(yd[2]), sh.at[k, 3], rh.at[k, 3], dn),
-        ]
-        return first, first_in, second, second_in
+            send(lo(yd[3]), lo(yd[3]), sh, rh.at[k, 2], up),
+            send(hi(yd[1]), hi(yd[1]), sh, rh.at[k, 2], dn),
+        ]
+        return first, first_in, second
 
     def k_copies(k):
         w = WIDTHS[k] // 2
         blk = lambda cc, yy: db.at[k, cc, yy, :, :, pl.ds(0, w)]
-        out = [send(blk(c, yd[d]), blk(c, yd[d]), sk.at[k, d], rk.at[k, d], sib) for d in range(NY)]
-        inn = [send(blk(oc, yd[d]), blk(oc, yd[d]), sk.at[k, d], rk.at[k, d], sib) for d in range(NY)]
-        return out, inn
+        return [send(blk(c, yd[d]), blk(c, yd[d]), sk, rk.at[k], sib) for d in range(NY)]
 
     def low(j0, j1, k):
         s0, w = STARTS[k], WIDTHS[k]
@@ -280,31 +272,32 @@
         for cp in z_copies(k):
             cp.start()
 
-    def s3(k):
-        s0, w = STARTS[k], WIDTHS[k]
-        for cp in z_copies(k):
-            cp.wait_recv()
-        t = zr[k, 0, :, 0:w // 2].astype(F32)
-        for d in range(1, NZ - 1):
-            t = t + zr[k, d, :, 0:w // 2].astype(F32)
-        g = zf[z, :, s0:s0 + w] + jnp.concatenate([t[0:8], t[8:16]], axis=1)
+    def step(k, g):
+        s0, w = STARTS[k], WIDTHS[k]
         a, b, dr = adam_rows(mv[:, s0:s0 + w], vv[:, s0:s0 + w], g)
         nm[:, s0:s0 + w] = a
         nv[:, s0:s0 + w] = b
         db[k, c, y, z, :, 0:w // 2] = jnp.concatenate([dr[:, :w // 2], dr[:, w // 2:]], axis=0).astype(BF16)
-        for cp in gz_copies(k)[0]:
+
+    def s3(k):
+        s0, w = STARTS[k], WIDTHS[k]
+        got(zr.at[k], rz.at[k])
+        t = zr[k, 0, :, 0:w // 2].astype(F32)
+        for d in range(1, NZ - 1):
+            t = t + zr[k, d, :, 0:w // 2].astype(F32)
+        step(k, zf[z, :, s0:s0 + w] + jnp.concatenate([t[0:8], t[8:16]], axis=1))
+        for cp in gz_copies(k):
             cp.start()
 
     def s4(k):
-        for cp in gz_copies(k)[1]:
-            cp.wait_recv()
+        got(zr.at[k], rg.at[k])
         for cp in gy_copies(k)[0]:
             cp.start()
-        k_copies(k)[0][0].start()
+        k_copies(k)[0].start()
 
     def s5(k):
-        _, first_in, second, _ = gy_copies(k)
-        out = k_copies(k)[0]
+        _, first_in, second = gy_copies(k)
+        out = k_copies(k)
         first_in[0].wait_recv()
         second[0].start()
         first_in[1].wait_recv()
@@ -313,14 +306,88 @@
         out[1].start()
 
     def s6(k):
-        for cp in gy_copies(k)[3]:
-            cp.wait_recv()
-        k_copies(k)[0][2].start()
+        got(db.at[k, c, 0], rh.at[k, 2])
+        k_copies(k)[2].start()
+
+    def qz_copies(k):
+        w = pl.ds(0, WIDTHS[k])
+        return [
+            send(qs.at[k, zd[d], :, w], qr.at[k, d - 1, :, w], sqz, rqz.at[k], dev(x, y, zd[d], c))
+            for d in range(1, NZ)
+        ]
+
+    def qy_copies(k):
+        w = pl.ds(0, WIDTHS[k] // 2)
+        return [
+            send(qys.at[k, j, :, w], qyr.at[k, j, :, w], sqy, rqy.at[k], dev(x, yo[j], z, c))
+            for j in range(3)
+        ]
+
+    def qg_copies(k):
+        mine = db.at[k, c, y, z, :, pl.ds(0, WIDTHS[k] // 2)]
+        return [send(mine, mine, sqg, rqg.at[k], dev(x, yd[d], z, c)) for d in range(1, NY)]
+
+    def qh_copies(k):
+        mine = db.at[k, c, :, z, :, pl.ds(0, WIDTHS[k] // 2)]
+        return [send(mine, mine, sqh, rqh.at[k], dev(x, y, zd[d], c)) for d in range(1, NZ)]
+
+    def got(ref, sem):
+        send(ref, ref, sem, sem, sib).wait_recv()
+
+    def left(ref, sem):
+        send(ref, ref, sem, sem, sib).wait_send()
+
+    def q1(k):
+        s0, w = STARTS[k], WIDTHS[k]
+        for h in range(2):
+            l = jnp.dot(ct[0, h].reshape(128, -1), u[0, :, s0:s0 + w], preferred_element_type=F32)
+            l += jnp.dot(ct[1, h].reshape(128, -1), u[1, :, s0:s0 + w], preferred_element_type=F32)
+            for zl in range(4):
+                part = jnp.concatenate([l[j * 32 + zl * 8:j * 32 + zl * 8 + 8] for j in range(NY)], axis=0)
+                qf[k, h * 4 + zl, :, 0:w] = part
+                qs[k, h * 4 + zl, :, 0:w] = part.astype(BF16)
+        for cp in qz_copies(k):
+            cp.start()
+
+    def halves(part):
+        w = part.shape[1] // 2
+        return jnp.concatenate([part[:, :w], part[:, w:]], axis=0).astype(BF16)
+
+    def q2(k):
+        w = WIDTHS[k]
+        got(qr.at[k], rqz.at[k])
+        g = qf[k, z, :, 0:w]
+        for d in range(NZ - 1):
+            g = g + qr[k, d, :, 0:w].astype(F32)
+        qf[k, 0, 0:8, 0:w] = g[24:32]
+        for j in range(3):
+            qys[k, j, :, 0:w // 2] = halves(g[j * 8:j * 8 + 8])
+        for cp in qy_copies(k):
+            cp.start()
+
+    def q3(k):
+        w = WIDTHS[k]
+        got(qyr.at[k], rqy.at[k])
+        t = qyr[k, 0, :, 0:w // 2].astype(F32)
+        for j in range(1, 3):
+            t = t + qyr[k, j, :, 0:w // 2].astype(F32)
+        step(k, qf[k, 0, 0:8, 0:w] + jnp.concatenate([t[0:8], t[8:16]], axis=1))
+        for cp in qg_copies(k):
+            cp.start()
+
+    def q4(k):
+        got(qyr.at[k], rqg.at[k])
+        for cp in qh_copies(k):
+            cp.start()
+
+    def q5(k):
+        got(zr.at[pl.ds(0, NY)], rqh.at[k])
+        for cp in k_copies(k):
+            cp.start()
 
     def s7(k):
         s0, w = STARTS[k], WIDTHS[k]
-        for cp in k_copies(k)[1]:
-            cp.wait_recv()
+        got(db.at[k, oc], rk.at[k])
         d_all = db[k, :, :, :, :, 0:w // 2].reshape(1024, w // 2)
         for s in range(2):
             o = s0 + s * (w // 2)
@@ -331,24 +398,23 @@
     lu.wait()
     cu_in.wait_recv()
     x_gathered(0)
-    for k in range(NCH):
+    for k in range(NQ, NCH):
         s0(k)
     x_gathered(1)
     lm.wait()
     lv.wait()
     basis_send()
 
-    stages = [s1, s2, s3, s4, s5, s6, s7]
-    order = []
+    p_stages = ((s1, P1), (s2, P2), (s3, P3), (s4, P4), (s5, P5), (s6, P6), (s7, 0.0))
+    q_stages = ((q1, Q1), (q2, Q2), (q3, Q3), (q4, Q4), (q5, Q5), (s7, 0.0))
+    order = [(BASIS_AT, 0, 0, lambda k: basis_columns())]
     for k in range(NCH):
-        t = PACE * k
-        for i in range(len(stages)):
-            order.append((t, -i, k))
-            t += LATENCY[i]
-    for n, (_, i, k) in enumerate(sorted(order)):
-        stages[-i](k)
-        if i == -1 and k == NCH - 1:
-            basis_columns()
+        t = Q_PACE * k if k < NQ else P_PACE * (k - NQ) + P_START
+        for i, (stage, latency) in enumerate(q_stages if k < NQ else p_stages):
+            order.append((t, -i, k, stage))
+            t += latency
+    for _, _, k, stage in sorted(order, key=lambda e: e[:3]):
+        stage(k)
 
     for p in range(2):
         for cp in cx[p]:
@@ -367,10 +433,17 @@
         for cp in cbs:
             cp.wait_send()
 
-    for k in range(NCH):
-        first, _, second, _ = gy_copies(k)
-        for cp in y_copies(k) + z_copies(k) + gz_copies(k)[0] + first + second + k_copies(k)[0]:
-            cp.wait_send()
+    rest = pl.ds(NQ, NCH - NQ)
+    left(ys.at[rest], sy)
+    left(zr.at[rest], sz)
+    left(zr.at[rest], sg)
+    left(db.at[rest, 0, pl.ds(0, 3)], sh)
+    left(db.at[:, 0], sk)
+    left(qr, sqz)
+    left(qyr, sqy)
+    left(qyr, sqg)
+    for k in range(NQ):
+        left(zr.at[pl.ds(0, NY)], sqh)
 
 
 def body(features, up_cotangent, proj_basis, first_moment, second_moment):
@@ -402,6 +475,11 @@
             pltpu.VMEM((NX - 1, NY, 32, tok), BF16),
             pltpu.VMEM((NY, 32, tok), BF16),
             pltpu.VMEM((2, 2, NY, 32, tok), BF16),
+            pltpu.VMEM((NQ, NZ, 32, WMAX), BF16),
+            pltpu.VMEM((NQ, NZ - 1, 32, WMAX), BF16),
+            pltpu.VMEM((NQ, NZ, 32, WMAX), F32),
+            pltpu.VMEM((NQ, 3, 16, WMAX // 2), BF16),
+            pltpu.VMEM((NQ, 3, 16, WMAX // 2), BF16),
             pltpu.VMEM((64, cols), F32),
             pltpu.VMEM((NCH, 3, 64, WMAX), BF16),
             pltpu.VMEM((NCH, 3, 64, WMAX), BF16),
@@ -413,8 +491,9 @@
             pltpu.VMEM((2, rows, 2 * rank), BF16),
             dma((KB,)), dma((KB,)), dma(()), dma((2,)),
             dma((2, 3)), dma((2, 3)), dma((2, 4)), dma((2, 2, 2)), dma(()), dma(()), dma((3,)), dma(()),
-            dma((NCH, 3)), dma((NCH, 3)), dma((NCH, 7)), dma((NCH, 7)), dma((NCH, 7)), dma((NCH, 7)),
-            dma((NCH, 4)), dma((NCH, 4)), dma((NCH, 4)), dma((NCH, 4)),
+            dma(()), dma((NCH, 3)), dma(()), dma((NCH,)), dma(()), dma((NCH,)),
+            dma(()), dma((NCH, 3)), dma(()), dma((NCH,)),
+            dma(()), dma((NQ,)), dma(()), dma((NQ,)), dma(()), dma((NQ,)), dma(()), dma((NQ,)),
         ],
         compiler_params=pltpu.CompilerParams(
             collective_id=0, has_side_effects=True, vmem_limit_bytes=56 * 2**20

time: 72.2 us -> 64.3 us (0.89)
  Pallas kernels: 69 us -> 61.1 us
    pallas_call x1, Pallas kernels: 69 us -> 61.1 us  [body(): pl.pallas_call(kernel, out_shape=(pltpu.VMEM((rows, cols), F32), pltpu.VM...]
where the time goes in v3:
time: 64.3 us; the launch traced here: 64.2 us
  Pallas kernels  61.1 us (95%)
  local copies, waits for them, and re-layouts  2.52 us (4%)
    pallas_call x1, Pallas kernels, body(): pl.pallas_call(kernel, out_shape=(pltpu.VMEM((rows, cols), F32), pltpu.VM...  61.1 us
    unnamed x3, local copies, waits for them, and re-layouts  2.52 us

profile of v3, /device:TPU:1, one launch (start us, length us, event | category | flops | bytes accessed | tf_op | source)
XLA Modules:
  0.0 64.2 jit_solution(3283754153718645941)
XLA Ops:
  0.6 61.1 %galore.1 = (f32[128,3584]{1,0:T(8,128)S(1)}, f32[8,3584]{1,0:T(8,128)S(1)}, f32[8,3584]{1,0:T(8,128)S(1)}) custom-call(bf16[512,2048]{1,0:T(8,128)(2,1)} %f_hbm.1, bf16[512,3584]{1,0:T(8,128)(2,1)} %u_hbm.1, bf16[2048,512]{1,0:T(8,128)(2,1)} %b_hbm.1, f32[8,3584]{1,0:T(8,128)} %m_hbm.1, f32[8,3584]{1,0:T(8,128)} %v_hbm.1), custom_call_target="tpu_custom_call" | custom-call | flops 4000000000 | bytes 12000000 | tf_op jit(solution)/shard_map/galore/pallas_call | solution.py:457
  61.7 1.2 %copy.11 = f32[128,3584]{1,0:T(8,128)} copy(f32[128,3584]{1,0:T(8,128)S(1)} %get-tuple-element.3) | data formatting | bytes 3670016
  62.9 0.6 %copy.12 = f32[8,3584]{1,0:T(8,128)} copy(f32[8,3584]{1,0:T(8,128)S(1)} %get-tuple-element.4) | data formatting | bytes 229376
  63.6 0.6 %copy.13 = f32[8,3584]{1,0:T(8,128)} copy(f32[8,3584]{1,0:T(8,128)S(1)} %get-tuple-element.5) | data formatting | bytes 229376

commit v4 on v3

--- a/solution.py
+++ b/solution.py
@@ -6,7 +6,7 @@
 from jax.sharding import PartitionSpec as P
 
 STEP = 10
-P_START, P_PACE, Q_PACE, BASIS_AT = 0.1, 0.8, 5.0, 12.0
+P_START, P_PACE, Q_PACE, BASIS_AT = 0.1, 0.8, 5.0, 20.0
 P1, P2, P3, P4, P5, P6 = 3.5, 5.5, 5.5, 4.0, 4.0, 2.0
 Q1, Q2, Q3, Q4, Q5 = 9.0, 3.5, 3.5, 9.0, 2.0
 PARTS = (pl.ds(0, 1), pl.ds(1, 3))
@@ -62,6 +62,8 @@
     zd = [lax.rem(z + d, NZ) for d in range(NZ)]
     yo = [yd[2], yd[1], yd[3], yd[0]]
     sib = dev(x, y, z, oc)
+    ydev = [dev(x, yd[d], z, c) for d in range(NY)]
+    zdev = [dev(x, y, zd[d], c) for d in range(NZ)]
 
     kw = fv.shape[2]
     lf_c = [pltpu.make_async_copy(f_hbm.at[:, pl.ds(k * kw, kw)], fv.at[k], ld_f.at[k]) for k in range(KB)]
@@ -107,7 +109,7 @@
     pl.semaphore_wait(bar, len(peers))
     cx = [
         [
-            send(xs.at[xd[d], sl], xr.at[d - 1, sl], sx.at[p, d - 1], rx.at[p, d - 1], dev(xd[d], y, z, c))
+            send(xs.at[xd[d], sl], xr.at[d - 1, sl], sx.at[p], rx.at[p], dev(xd[d], y, z, c))
             for d in range(1, NX)
         ]
         for p, sl in enumerate(PARTS)
@@ -127,8 +129,7 @@
         return [send(qv.at[sl], ct.at[c, hx, sl], sq.at[p, d], rq.at[p, c, hx], dev(xd[d], y, z, cq)) for d in range(NX)]
 
     def x_reduce(p):
-        for cp in cx[p]:
-            cp.wait_recv()
+        got(xr.at[:, PARTS[p]], rx.at[p])
         for j in (0,) if p == 0 else (1, 2, 3):
             q = pt[x, yo[j]]
             for d in range(NX - 1):
@@ -190,21 +191,21 @@
 
     def y_copies(k):
         w = pl.ds(0, WIDTHS[k])
-        up, dn = dev(x, yd[1], z, c), dev(x, yd[3], z, c)
+        up, dn = ydev[1], ydev[3]
         to = (up, up, dn) if k % 2 == 0 else (dn, dn, up)
         return [send(ys.at[k, i, :, w], yr.at[k, i, :, w], sy, ry.at[k, i], to[i]) for i in range(3)]
 
     def z_copies(k):
         w = WIDTHS[k] // 2
         return [
-            send(zs.at[k, zd[d], :, pl.ds(0, w)], zr.at[k, d - 1, :, pl.ds(0, w)], sz, rz.at[k], dev(x, y, zd[d], c))
+            send(zs.at[k, zd[d], :, pl.ds(0, w)], zr.at[k, d - 1, :, pl.ds(0, w)], sz, rz.at[k], zdev[d])
             for d in range(1, NZ)
         ]
 
     def gz_copies(k):
         w = WIDTHS[k] // 2
         mine = db.at[k, c, y, z, :, pl.ds(0, w)]
-        out = [send(mine, mine, sg, rg.at[k], dev(x, y, zd[d], c)) for d in range(1, NZ)]
+        out = [send(mine, mine, sg, rg.at[k], zdev[d]) for d in range(1, NZ)]
         return out
 
     def gy_copies(k):
@@ -212,7 +213,7 @@
         blk = lambda yy: db.at[k, c, yy, :, :, pl.ds(0, w)]
         lo = lambda yy: db.at[k, c, yy, pl.ds(0, 4), :, pl.ds(0, w)]
         hi = lambda yy: db.at[k, c, yy, pl.ds(4, 4), :, pl.ds(0, w)]
-        up, dn = dev(x, yd[1], z, c), dev(x, yd[3], z, c)
+        up, dn = ydev[1], ydev[3]
         first = [
             send(blk(y), blk(y), sh, rh.at[k, 0], up),
             send(blk(y), blk(y), sh, rh.at[k, 1], dn),
@@ -281,7 +282,7 @@
 
     def s3(k):
         s0, w = STARTS[k], WIDTHS[k]
-        got(zr.at[k], rz.at[k])
+        got(zr.at[k, :, :, pl.ds(0, w // 2)], rz.at[k])
         t = zr[k, 0, :, 0:w // 2].astype(F32)
         for d in range(1, NZ - 1):
             t = t + zr[k, d, :, 0:w // 2].astype(F32)
@@ -290,7 +291,7 @@
             cp.start()
 
     def s4(k):
-        got(zr.at[k], rg.at[k])
+        got(zr.at[k, :, :, pl.ds(0, WIDTHS[k] // 2)], rg.at[k])
         for cp in gy_copies(k)[0]:
             cp.start()
         k_copies(k)[0].start()
@@ -306,30 +307,30 @@
         out[1].start()
 
     def s6(k):
-        got(db.at[k, c, 0], rh.at[k, 2])
+        got(db.at[k, c, 0, :, :, pl.ds(0, WIDTHS[k] // 2)], rh.at[k, 2])
         k_copies(k)[2].start()
 
     def qz_copies(k):
         w = pl.ds(0, WIDTHS[k])
         return [
-            send(qs.at[k, zd[d], :, w], qr.at[k, d - 1, :, w], sqz, rqz.at[k], dev(x, y, zd[d], c))
+            send(qs.at[k, zd[d], :, w], qr.at[k, d - 1, :, w], sqz, rqz.at[k], zdev[d])
             for d in range(1, NZ)
         ]
 
     def qy_copies(k):
         w = pl.ds(0, WIDTHS[k] // 2)
         return [
-            send(qys.at[k, j, :, w], qyr.at[k, j, :, w], sqy, rqy.at[k], dev(x, yo[j], z, c))
+            send(qys.at[k, j, :, w], qyr.at[k, j, :, w], sqy, rqy.at[k], (ydev[2], ydev[1], ydev[3])[j])
             for j in range(3)
         ]
 
     def qg_copies(k):
         mine = db.at[k, c, y, z, :, pl.ds(0, WIDTHS[k] // 2)]
-        return [send(mine, mine, sqg, rqg.at[k], dev(x, yd[d], z, c)) for d in range(1, NY)]
+        return [send(mine, mine, sqg, rqg.at[k], ydev[d]) for d in range(1, NY)]
 
     def qh_copies(k):
         mine = db.at[k, c, :, z, :, pl.ds(0, WIDTHS[k] // 2)]
-        return [send(mine, mine, sqh, rqh.at[k], dev(x, y, zd[d], c)) for d in range(1, NZ)]
+        return [send(mine, mine, sqh, rqh.at[k], zdev[d]) for d in range(1, NZ)]
 
     def got(ref, sem):
         send(ref, ref, sem, sem, sib).wait_recv()
@@ -355,7 +356,7 @@
 
     def q2(k):
         w = WIDTHS[k]
-        got(qr.at[k], rqz.at[k])
+        got(qr.at[k, :, :, pl.ds(0, w)], rqz.at[k])
         g = qf[k, z, :, 0:w]
         for d in range(NZ - 1):
             g = g + qr[k, d, :, 0:w].astype(F32)
@@ -367,7 +368,7 @@
 
     def q3(k):
         w = WIDTHS[k]
-        got(qyr.at[k], rqy.at[k])
+        got(qyr.at[k, :, :, pl.ds(0, w // 2)], rqy.at[k])
         t = qyr[k, 0, :, 0:w // 2].astype(F32)
         for j in range(1, 3):
             t = t + qyr[k, j, :, 0:w // 2].astype(F32)
@@ -376,18 +377,18 @@
             cp.start()
 
     def q4(k):
-        got(qyr.at[k], rqg.at[k])
+        got(qyr.at[k, :, :, pl.ds(0, WIDTHS[k] // 2)], rqg.at[k])
         for cp in qh_copies(k):
             cp.start()
 
     def q5(k):
-        got(zr.at[pl.ds(0, NY)], rqh.at[k])
+        got(db.at[k, c, :, pl.ds(0, NZ - 1), :, pl.ds(0, WIDTHS[k] // 2)], rqh.at[k])
         for cp in k_copies(k):
             cp.start()
 
     def s7(k):
         s0, w = STARTS[k], WIDTHS[k]
-        got(db.at[k, oc], rk.at[k])
+        got(db.at[k, oc, :, :, :, pl.ds(0, w // 2)], rk.at[k])
         d_all = db[k, :, :, :, :, 0:w // 2].reshape(1024, w // 2)
         for s in range(2):
             o = s0 + s * (w // 2)
@@ -417,8 +418,7 @@
         stage(k)
 
     for p in range(2):
-        for cp in cx[p]:
-            cp.wait_send()
+        left(xr.at[:, PARTS[p]], sx.at[p])
         for d in range(1, NX):
             q_copies(p)[d].wait_send()
 
@@ -433,17 +433,19 @@
         for cp in cbs:
             cp.wait_send()
 
-    rest = pl.ds(NQ, NCH - NQ)
-    left(ys.at[rest], sy)
-    left(zr.at[rest], sz)
-    left(zr.at[rest], sg)
-    left(db.at[rest, 0, pl.ds(0, 3)], sh)
-    left(db.at[:, 0], sk)
-    left(qr, sqz)
-    left(qyr, sqy)
-    left(qyr, sqg)
-    for k in range(NQ):
-        left(zr.at[pl.ds(0, NY)], sqh)
+    for k in range(NCH):
+        w, half = pl.ds(0, WIDTHS[k]), pl.ds(0, WIDTHS[k] // 2)
+        if k < NQ:
+            left(qr.at[k, :, :, w], sqz)
+            left(qyr.at[k, :, :, half], sqy)
+            left(qyr.at[k, :, :, half], sqg)
+            left(db.at[k, 0, :, pl.ds(0, NZ - 1), :, half], sqh)
+        else:
+            left(ys.at[k, :, :, w], sy)
+            left(zr.at[k, :, :, half], sz)
+            left(zr.at[k, :, :, half], sg)
+            left(db.at[k, 0, pl.ds(0, 3), :, :, half], sh)
+        left(db.at[k, 0, :, :, :, half], sk)
 
 
 def body(features, up_cotangent, proj_basis, first_moment, second_moment):
@@ -490,7 +492,7 @@
             pltpu.VMEM((rows, rank), BF16),
             pltpu.VMEM((2, rows, 2 * rank), BF16),
             dma((KB,)), dma((KB,)), dma(()), dma((2,)),
-            dma((2, 3)), dma((2, 3)), dma((2, 4)), dma((2, 2, 2)), dma(()), dma(()), dma((3,)), dma(()),
+            dma((2,)), dma((2,)), dma((2, 4)), dma((2, 2, 2)), dma(()), dma(()), dma((3,)), dma(()),
             dma(()), dma((NCH, 3)), dma(()), dma((NCH,)), dma(()), dma((NCH,)),
             dma(()), dma((NCH, 3)), dma(()), dma((NCH,)),
             dma(()), dma((NQ,)), dma(()), dma((NQ,)), dma(()), dma((NQ,)), dma(()), dma((NQ,)),

time: 64.3 us -> 64.3 us (level)
  no operation moved by 1% of the time
where the time goes in v4:
time: 64.3 us; the launch traced here: 64.2 us
  Pallas kernels  61 us (95%)
  local copies, waits for them, and re-layouts  2.52 us (4%)
    pallas_call x1, Pallas kernels, body(): pl.pallas_call(kernel, out_shape=(pltpu.VMEM((rows, cols), F32), pltpu.VM...  61 us
    unnamed x3, local copies, waits for them, and re-layouts  2.52 us

profile of v4, /device:TPU:1, one launch (start us, length us, event | category | flops | bytes accessed | tf_op | source)
XLA Modules:
  0.0 64.2 jit_solution(11018686240921377192)
XLA Ops:
  0.6 61.0 %galore.1 = (f32[128,3584]{1,0:T(8,128)S(1)}, f32[8,3584]{1,0:T(8,128)S(1)}, f32[8,3584]{1,0:T(8,128)S(1)}) custom-call(bf16[512,2048]{1,0:T(8,128)(2,1)} %f_hbm.1, bf16[512,3584]{1,0:T(8,128)(2,1)} %u_hbm.1, bf16[2048,512]{1,0:T(8,128)(2,1)} %b_hbm.1, f32[8,3584]{1,0:T(8,128)} %m_hbm.1, f32[8,3584]{1,0:T(8,128)} %v_hbm.1), custom_call_target="tpu_custom_call" | custom-call | flops 4000000000 | bytes 12000000 | tf_op jit(solution)/shard_map/galore/pallas_call | solution.py:459
  61.7 1.2 %copy.11 = f32[128,3584]{1,0:T(8,128)} copy(f32[128,3584]{1,0:T(8,128)S(1)} %get-tuple-element.3) | data formatting | bytes 3670016
  62.9 0.6 %copy.12 = f32[8,3584]{1,0:T(8,128)} copy(f32[8,3584]{1,0:T(8,128)S(1)} %get-tuple-element.4) | data formatting | bytes 229376
  63.5 0.6 %copy.13 = f32[8,3584]{1,0:T(8,128)} copy(f32[8,3584]{1,0:T(8,128)S(1)} %get-tuple-element.5) | data formatting | bytes 229376
